TPU v7x, 32 devices: a whole 2x2x4 slice. The times are simulated.
32 devices in a mesh: groups: 2 (over y), src: 8 (over z, x), own: 2 (over core).
Axes of the slice: x: 2, y: 2, z: 4, core: 2. Of those that a mesh axis runs over, the one named last changes fastest.
Arguments:
- embeddings: bfloat16 [32768, 768], P(('groups', 'src', 'own')), parts along dimension 0, may hold values from -100 to 100
- cluster_id: int32 [32768], P(('groups', 'src', 'own')), parts along dimension 0, may hold values from 0 to 31, as said below
- member_rank: int32 [32768], P(('groups', 'src', 'own')), parts along dimension 0, may hold values from 0 to 1023, as said below
Outputs:
- best_similarity: float32 [32768], P(('groups', 'src', 'own')), parts along dimension 0
There are 2 independent parts, one for each index of `groups`. A program takes and returns all parts, laid end to end along the dimension named above; each array names one. Nothing has to cross between parts.
Inputs may be any that keep to these rules, and one draw needn't show every extreme that they name: `cluster_id`: cluster c is owned by device c mod 16 of the group (src major, own minor). Every device holds exactly 64 rows of the clusters of each owner. Cluster sizes are uneven: in every draw the rows of some owner all belong to one of its clusters. `member_rank`: the rows of one cluster carry the ranks 0 to its size - 1, each once. A cluster has at most 1024 rows, and in every draw one cluster has exactly that many.
All inputs are finite; a program needn't handle non-finite values.
Results may differ from a plain program's by a relative error of at most 0.0009.
Values may be sent and summed in bfloat16 or wider, within the bound.
A program may use at most 64 MiB of HBM per device.

v0:
```python
import jax
import jax.numpy as jnp
from jax import lax
from jax.sharding import PartitionSpec as P

EPS = 1e-06


def shards(embeddings, cluster_id, member_rank):
    rows_dev = embeddings.shape[0]
    width = embeddings.shape[1]
    src_count = lax.axis_size("src")
    own_count = lax.axis_size("own")
    owners = src_count * own_count
    slot_rows = rows_dev // owners
    capacity = owners * slot_rows
    values = embeddings.astype(jnp.float32)
    normalized = (values / jnp.sqrt(jnp.sum(values * values, axis=1, keepdims=True) + EPS)).astype(
        jnp.bfloat16
    )
    owner = cluster_id % owners
    onehot = (owner[:, None] == jnp.arange(owners, dtype=jnp.int32)[None, :]).astype(jnp.int32)
    before = jnp.sum(jnp.cumsum(onehot, axis=0) * onehot, axis=1) - 1
    target = owner * slot_rows + before
    outgoing = jnp.zeros((capacity, width), jnp.bfloat16).at[target].set(normalized)
    ids_out = jnp.full((capacity,), -1, jnp.int32).at[target].set(cluster_id)
    rank_out = jnp.full((capacity,), -1, jnp.int32).at[target].set(member_rank)
    arrived = (
        lax.all_to_all(
            outgoing.reshape(owners, slot_rows, width),
            ("src", "own"),
            split_axis=0,
            concat_axis=0,
            tiled=True,
        ),
        lax.all_to_all(
            ids_out.reshape(owners, slot_rows),
            ("src", "own"),
            split_axis=0,
            concat_axis=0,
            tiled=True,
        ),
        lax.all_to_all(
            rank_out.reshape(owners, slot_rows),
            ("src", "own"),
            split_axis=0,
            concat_axis=0,
            tiled=True,
        ),
    )
    rows_in = arrived[0].reshape(capacity, width)
    ids_in = arrived[1].reshape(capacity)
    rank_in = arrived[2].reshape(capacity)
    block_rows = 512

    def score_block(pieces):
        query_rows, query_ids, query_rank = pieces
        similar = jnp.einsum("qd,kd->qk", query_rows, rows_in, preferred_element_type=jnp.float32)
        earlier = (query_ids[:, None] == ids_in[None, :]) & (rank_in[None, :] < query_rank[:, None])
        return jnp.max(jnp.where(earlier, similar, -1.0), axis=1)

    largest = lax.map(
        score_block,
        (
            rows_in.reshape(-1, block_rows, width),
            ids_in.reshape(-1, block_rows),
            rank_in.reshape(-1, block_rows),
        ),
    )
    returned = lax.all_to_all(
        largest.reshape(owners, slot_rows), ("src", "own"), split_axis=0, concat_axis=0, tiled=True
    )
    return returned.reshape(capacity)[target]


def solution(mesh):
    in_specs = (
        P(("groups", "src", "own"), None),
        P(("groups", "src", "own")),
        P(("groups", "src", "own")),
    )
    out_specs = P(("groups", "src", "own"))
    return jax.shard_map(shards, mesh=mesh, in_specs=in_specs, out_specs=out_specs, check_vma=False)
```

profile of v0, /device:TPU:0, one launch (start us, length us, event | category | flops | bytes accessed | tf_op | source)
XLA Modules:
  0.0 104.8 jit_solution(13811751167042159855)
XLA Ops:
  0.0 0.0 copy-start
  0.0 0.8 add_select_fusion
  0.8 4.5 %reduce-window.6 = s32[16,8,128]{2,1,0:T(8,128)S(1)} reduce-window(s32[16,8,128]{2,1,0:T(8,128)S(1)} %fusion.11, s32[]{:T(128)} %constant.31.clone.1), window={size=1x1x128 pad=0_0x0_0x127_0}, to_apply=%region_0.0 | reduce-window | flops 2080768 | bytes 131076 | tf_op jit(solution)/shard_map/reduce-window
  5.3 0.1 slice.10
  5.4 0.1 copy.8
  5.6 0.1 copy.9
  5.7 0.1 broadcast_add_fusion
  5.8 0.7 broadcast_clamp_fusion
  6.5 4.5 %scatter_custom_fusion = s32[1024]{0:T(1024)S(1)} fusion(s32[1024]{0:T(1024)S(1)} %get-tuple-element.65, s32[1024]{0:T(1024)} %param.6, s32[]{:T(128)} %constant.49.clone.1), kind=kCustom, calls=%fused_computation.33 | custom fusion | bytes 4608 | tf_op jit(solution)/shard_map/scatter | solution.py:26
  11.0 0.7 all_to_all.25
  11.6 7.4 %all-to-all-start = ((s32[16,1,64]{2,1,0:T(1,128)}), s32[16,1,64]{2,1,0:T(1,128)S(1)}, u32[]{:S(2)}, u32[]{:S(2)}) async-start(s32[16,1,64]{2,1,0:T(1,128)} %all_to_all.25), calls=%async_computation | async-start | bytes 16384 | tf_op jit(solution)/shard_map/all_to_all | solution.py:36
  19.0 1.8 %fusion.3 = f32[1024]{0:T(1024)S(1)} fusion(bf16[1024,768]{1,0:T(8,128)(2,1)} %param.5), kind=kLoop, calls=%fused_computation.12 | loop fusion | flops 2358272 | bytes 1576960 | tf_op jit(solution)/shard_map/reduce_sum | solution.py:18
  20.8 4.5 %scatter_custom_fusion.1 = s32[1024]{0:T(1024)S(1)} fusion(s32[1024]{0:T(1024)S(1)} %get-tuple-element.65, s32[1024]{0:T(1024)} %param.7, s32[]{:T(128)} %constant.49.clone.1), kind=kCustom, calls=%fused_computation.31 | custom fusion | bytes 4608 | tf_op jit(solution)/shard_map/scatter | solution.py:27
  25.3 0.7 all_to_all.28
  26.0 0.0 all-to-all-done
  26.0 0.0 copy-start.1
  26.0 6.0 %all-to-all-start.1 = ((s32[16,1,64]{2,1,0:T(1,128)}), s32[16,1,64]{2,1,0:T(1,128)S(1)}, u32[]{:S(2)}, u32[]{:S(2)}) async-start(s32[16,1,64]{2,1,0:T(1,128)} %all_to_all.28), calls=%async_computation.1 | async-start | bytes 16384 | tf_op jit(solution)/shard_map/all_to_all | solution.py:43
  32.0 0.0 copy-done
  32.0 6.9 %scatter_custom_fusion.2 = bf16[1024,768]{1,0:T(8,128)(2,1)} fusion(s32[1024]{0:T(1024)S(1)} %get-tuple-element.65, bf16[1024,768]{1,0:T(8,128)(2,1)S(1)} %copy-done, f32[1024]{0:T(1024)S(1)} %add_sqrt_fusion, bf16[]{:T(256)} %constant.45.clone.1), kind=kCustom, calls=%fused_computation.14 | custom fusion | flops 2359296 | bytes 3149826 | tf_op jit(solution)/shard_map/scatter | solution.py:25
  38.9 0.0 all-to-all-done.1
  38.9 0.0 copy-start.2
  38.9 6.0 %all-to-all-start.2 = ((bf16[16,64,768]{2,1,0:T(8,128)(2,1)}), bf16[16,64,768]{2,1,0:T(8,128)(2,1)S(1)}, u32[]{:S(2)}, u32[]{:S(2)}) async-start(bf16[16,64,768]{2,1,0:T(8,128)(2,1)} %bitcast.9), calls=%async_computation.2 | async-start | bytes 3145728 | tf_op jit(solution)/shard_map/all_to_all | solution.py:29
  44.9 0.5 broadcast.66
  45.4 0.7 reduce.9
  46.1 0.1 reshape_reshape.9
  46.2 0.7 reduce.10
  46.8 0.1 reshape_reshape.10
  46.9 0.0 copy-done.2
  46.9 0.1 lt.45
  47.0 0.0 copy-done.1
  47.0 0.1 eq.66
  47.1 29.8 %all-to-all-done.2 = bf16[16,64,768]{2,1,0:T(8,128)(2,1)S(1)} async-done(((bf16[16,64,768]{2,1,0:T(8,128)(2,1)}), bf16[16,64,768]{2,1,0:T(8,128)(2,1)S(1)}, u32[]{:S(2)}, u32[]{:S(2)}) %all-to-all-start.2) | async-done | bytes 1572896 | tf_op jit(solution)/shard_map/all_to_all | solution.py:29
  76.9 2.4 %while.11 = (s32[]{:T(128)}, f32[2,512]{1,0:T(2,128)S(1)}, s32[2,512]{1,0:T(2,128)S(1)}, s32[16,64]{1,0:T(8,128)}, s32[16,64]{1,0:T(8,128)}, /*index=5*/s32[2,51...) while((s32[]{:T(128)}, f32[2,512]{1,0:T(2,128)S(1)}, ...), condition=%wide.wide.region_9.10_spmd, body=%wide.wide.region_7.9_spmd.sunk | while | flops 807927296 | bytes 2386057 | solution.py:62
  76.9 1.2 %select_reduce_fusion.3 = f32[512]{0:T(512)S(1)} fusion(bf16[1024,768]{1,0:T(8,128)(2,1)S(1)} %get-tuple-element.199, s32[1024]{0:T(1024)S(1)} %get-tuple-element.200, s32[1024]{0:T(1024)S(1)} %get-tuple-element.201, s32[512]{0:T(512)S(1)} %bitcast.52, s32[512]{0:T(512)S(1)} %bitcast.53, bf16[2,512,768]{2,1,0:T(8,128)(2,1)S(1)} %bitcast.45, ...), kind=kOutput, calls=%fused_computation.4.clone.clone.1 | convolution fusion | flops 807927296 | bytes 2373636 | tf_op jit(solution)/shard_map/while/body/eval_jaxpr/qd,kd->qk/dot_general | solution.py:58
  78.1 1.2 %select_reduce_fusion.3 = f32[512]{0:T(512)S(1)} fusion(bf16[1024,768]{1,0:T(8,128)(2,1)S(1)} %get-tuple-element.199, s32[1024]{0:T(1024)S(1)} %get-tuple-element.200, s32[1024]{0:T(1024)S(1)} %get-tuple-element.201, s32[512]{0:T(512)S(1)} %bitcast.52, s32[512]{0:T(512)S(1)} %bitcast.53, bf16[2,512,768]{2,1,0:T(8,128)(2,1)S(1)} %bitcast.45, ...), kind=kOutput, calls=%fused_computation.4.clone.clone.1 | convolution fusion | flops 807927296 | bytes 2373636 | tf_op jit(solution)/shard_map/while/body/eval_jaxpr/qd,kd->qk/dot_general | solution.py:58
  79.3 0.1 all_to_all.32
  79.4 15.3 %all_to_all.38 = f32[16,1,64]{2,1,0:T(1,128)S(1)} all-to-all(f32[16,1,64]{2,1,0:T(1,128)S(1)} %all_to_all.32), channel_id=1, replica_groups=mesh['groups'=2,'src'=8,'own'=2] {'src','own'}, dimensions={0} | all-to-all | bytes 8192 | tf_op jit(solution)/shard_map/all_to_all | solution.py:70
  94.7 0.5 broadcast.68
  95.2 0.7 reduce.11
  95.9 0.1 reshape.55
  96.0 8.8 %gather_fusion = f32[1024]{0:T(1024)} fusion(f32[1024]{0:T(1024)S(1)} %reshape.55, s32[1024]{0:T(1024)S(1)} %get-tuple-element.64), kind=kCustom, calls=%fused_computation | custom fusion | bytes 12288 | tf_op jit(solution)/shard_map/gather | solution.py:73
  (10 shorter events, 0.2 us)
Async XLA Ops:
  0.0 32.0 %copy-start = (bf16[1024,768]{1,0:T(8,128)(2,1)S(1)}, bf16[1024,768]{1,0:T(8,128)(2,1)}, u32[]{:S(2)}) copy-start(bf16[1024,768]{1,0:T(8,128)(2,1)} %param.5) | copy-start | bytes 4718596
  11.6 14.3 %all-to-all-start = ((s32[16,1,64]{2,1,0:T(1,128)}), s32[16,1,64]{2,1,0:T(1,128)S(1)}, u32[]{:S(2)}, u32[]{:S(2)}) async-start(s32[16,1,64]{2,1,0:T(1,128)} %all_to_all.25), calls=%async_computation | async-start | bytes 16384 | tf_op jit(solution)/shard_map/all_to_all | solution.py:36
  26.0 21.0 %copy-start.1 = (s32[16,1,64]{2,1,0:T(1,128)}, s32[16,1,64]{2,1,0:T(1,128)S(1)}, u32[]{:S(2)}) copy-start(s32[16,1,64]{2,1,0:T(1,128)S(1)} %all-to-all-done) | copy-start | bytes 12292
  26.0 12.9 %all-to-all-start.1 = ((s32[16,1,64]{2,1,0:T(1,128)}), s32[16,1,64]{2,1,0:T(1,128)S(1)}, u32[]{:S(2)}, u32[]{:S(2)}) async-start(s32[16,1,64]{2,1,0:T(1,128)} %all_to_all.28), calls=%async_computation.1 | async-start | bytes 16384 | tf_op jit(solution)/shard_map/all_to_all | solution.py:43
  38.9 8.0 %copy-start.2 = (s32[16,1,64]{2,1,0:T(1,128)}, s32[16,1,64]{2,1,0:T(1,128)S(1)}, u32[]{:S(2)}) copy-start(s32[16,1,64]{2,1,0:T(1,128)S(1)} %all-to-all-done.1) | copy-start | bytes 12292
  38.9 38.0 %all-to-all-start.2 = ((bf16[16,64,768]{2,1,0:T(8,128)(2,1)}), bf16[16,64,768]{2,1,0:T(8,128)(2,1)S(1)}, u32[]{:S(2)}, u32[]{:S(2)}) async-start(bf16[16,64,768]{2,1,0:T(8,128)(2,1)} %bitcast.9), calls=%async_computation.2 | async-start | bytes 3145728 | tf_op jit(solution)/shard_map/all_to_all | solution.py:29
where the time goes:
time: 105 us
  waiting for transfers between devices  29.8 us (28%)
  local copies, waits for them, and re-layouts  21 us (20%)
  starting transfers between devices  19.4 us (18%)
  other arithmetic  16.8 us (16%)
  blocking collectives  15.3 us (15%)
  matrix products  2.31 us (2%)
    all_to_all x1, waiting for transfers between devices, shards(): lax.all_to_all(outgoing.reshape(owners, slot_rows, width), ('src', 'own')...  29.8 us
    all_to_all x1, blocking collectives, shards(): lax.all_to_all(largest.reshape(owners, slot_rows), ('src', 'own'), split_...  15.3 us
    gather x1, local copies, waits for them, and re-layouts, shards(): return returned.reshape(capacity)[target]  8.83 us
    all_to_all x1, starting transfers between devices, shards(): lax.all_to_all(ids_out.reshape(owners, slot_rows), ('src', 'own'), split_...  7.36 us
    scatter x1, other arithmetic, shards(): jnp.zeros((capacity, width), jnp.bfloat16).at[target].set(normalized)  6.87 us
    all_to_all x1, starting transfers between devices, shards(): lax.all_to_all(rank_out.reshape(owners, slot_rows), ('src', 'own'), split...  6.01 us
    all_to_all x1, starting transfers between devices, shards(): lax.all_to_all(outgoing.reshape(owners, slot_rows, width), ('src', 'own')...  6.01 us
    another operation x3, other arithmetic  4.63 us
  transfers between devices with their start and end apart: 3, of which 1 were waited for; matrix products, arithmetic and copies ran while one was open for 15% of the time, Pallas kernels for 0%

commit v1 on v0

v1 whole, which is shorter than its diff:
```python
import functools

import jax
import jax.numpy as jnp
from jax import lax
from jax.experimental import pallas as pl
from jax.experimental.pallas import tpu as pltpu
from jax.sharding import PartitionSpec as P

EPS = 1e-06
MESH = pl.DeviceIdType.MESH
GROUP = 256
GAP = 4096.0
SELF = 1


def log2(n):
    assert n & (n - 1) == 0
    return n.bit_length() - 1


def kernel(
    n_src, n_own, slot, emb_hbm, cid_ref, rank_ref, out_ref,
    emb, stage, recv, mstage, mrecv, rstage, rrecv, keyrow, baserow, keycol, best,
    in_sem, d_send, d_recv, m_send, m_recv, r_send, r_recv,
):
    n = n_src * n_own
    h = n_src // 2
    rows, width = emb.shape
    chunks = rows // 128
    per_group = GROUP // slot
    groups = n // per_group
    s = lax.axis_index("src")
    c = lax.axis_index("own")
    half, off = s // h, s % h

    def place(t, sign):
        near, q = t % 2, t // 2
        j, cc = q // n_own, q % n_own
        side = half if near else 1 - half
        return {
            "src": side * h + (off + h + sign * j) % h,
            "own": (c + n_own + sign * cc) % n_own,
        }

    others = [t for t in range(n) if t != SELF]
    load = pltpu.make_async_copy(emb_hbm, emb, in_sem)
    load.start()
    barrier = pltpu.get_barrier_semaphore()
    for t in others:
        pl.semaphore_signal(barrier, inc=1, device_id=place(t, 1), device_id_type=MESH)

    cid = cid_ref[...]
    owner = cid & (n - 1)
    ds, dc = owner >> log2(n_own), owner & (n_own - 1)
    near = jnp.where((ds >> log2(h)) == half, 1, 0)
    step = 2 * ((((ds & (h - 1)) - off) & (h - 1)) * n_own + ((dc - c) & (n_own - 1))) + near
    upper = jnp.where(
        lax.broadcasted_iota(jnp.int32, (128, 128), 0) < lax.broadcasted_iota(jnp.int32, (128, 128), 1),
        1.0, 0.0,
    ).astype(jnp.bfloat16)
    which = lax.broadcasted_iota(jnp.int32, (n, 128), 0)
    hot = [jnp.where(which == step[k : k + 1, :], 1.0, 0.0) for k in range(chunks)]
    within = jnp.dot(
        jnp.concatenate(hot, axis=0).astype(jnp.bfloat16), upper, preferred_element_type=jnp.float32
    )
    seen = jnp.zeros((n, 1), jnp.float32)
    pos = []
    for k in range(chunks):
        pos.append(jnp.sum(hot[k] * (within[k * n : (k + 1) * n] + seen), axis=0, keepdims=True))
        seen = seen + jnp.sum(hot[k], axis=1, keepdims=True)
    pos = jnp.concatenate(pos, axis=1).astype(jnp.int32)

    def as_row(x):
        return jnp.concatenate([x[k : k + 1, :] for k in range(chunks)], axis=1)

    step_row = as_row(step)
    target = step_row * slot + pos
    rank = rank_ref[...]
    meta = jnp.concatenate(
        [as_row((cid >> log2(n)) + 1), as_row(rank >> 5), as_row(rank & 31), jnp.zeros((5, rows), jnp.int32)],
        axis=0,
    ).astype(jnp.float32).astype(jnp.bfloat16)
    mstage[...] = jnp.zeros_like(mstage)
    mrecv[SELF] = jnp.zeros_like(mrecv[SELF])

    def data_copy(t):
        part = pl.ds(t * slot, slot)
        return pltpu.make_async_remote_copy(
            src_ref=stage.at[part], dst_ref=recv.at[part], send_sem=d_send.at[t], recv_sem=d_recv.at[t],
            device_id=place(t, 1), device_id_type=MESH,
        )

    def meta_copy(t):
        return pltpu.make_async_remote_copy(
            src_ref=mstage.at[t], dst_ref=mrecv.at[t], send_sem=m_send.at[t], recv_sem=m_recv.at[t],
            device_id=place(t, 1), device_id_type=MESH,
        )

    def result_copy(t):
        return pltpu.make_async_remote_copy(
            src_ref=rstage.at[t], dst_ref=rrecv.at[t], send_sem=r_send.at[t], recv_sem=r_recv.at[t],
            device_id=place(t, -1), device_id_type=MESH,
        )

    load.wait()
    for g in range(groups):
        slots = lax.broadcasted_iota(jnp.int32, (GROUP, rows), 0) + g * GROUP
        pick = jnp.where(slots == target, 1.0, 0.0).astype(jnp.bfloat16)
        picked = jnp.dot(pick, emb[...], preferred_element_type=jnp.float32)
        scale = 1.0 / jnp.sqrt(jnp.sum(picked * picked, axis=1, keepdims=True) + EPS)
        normalized = (picked * scale).astype(jnp.bfloat16)
        stage[pl.ds(g * GROUP, GROUP), :] = normalized
        about = lax.dot_general(
            meta, pick, (((1,), (1,)), ((), ())), preferred_element_type=jnp.float32
        )
        about = jnp.concatenate([about[0:1], about[1:2] * 32.0 + about[2:3]], axis=0)
        for u in range(per_group):
            t = g * per_group + u
            piece = about[:, u * slot : (u + 1) * slot]
            if t == SELF:
                recv[pl.ds(t * slot, slot), :] = normalized[u * slot : (u + 1) * slot]
                mrecv[t, :, 0:slot] = piece
            else:
                mstage[t, :, 0:slot] = piece
        if g == 0:
            pl.semaphore_wait(barrier, n - 1)
        for u in range(per_group):
            t = g * per_group + u
            if t != SELF:
                meta_copy(t).start()
                data_copy(t).start()

    best[...] = jnp.full_like(best, -1.0)

    def score(k, q):
        similar = lax.dot_general(
            recv[pl.ds(k * GROUP, GROUP), :], recv[pl.ds(q * GROUP, GROUP), :],
            (((1,), (1,)), ((), ())), preferred_element_type=jnp.float32,
        )
        key = keycol[k]
        key = jnp.concatenate([key] * (GROUP // 128), axis=1)
        earlier = (key < keyrow[q]) & (key >= baserow[q])
        best[q] = jnp.maximum(
            best[q], jnp.max(jnp.where(earlier, similar, -1.0), axis=0, keepdims=True)
        )

    for g in range(groups):
        pieces = []
        for u in range(per_group):
            t = g * per_group + u
            if t != SELF:
                meta_copy(t).wait_recv()
            pieces.append(mrecv[t, :, 0:slot])
        pieces = jnp.concatenate(pieces, axis=1)
        base = pieces[0:1] * GAP
        key = base + pieces[1:2]
        baserow[g] = base
        keyrow[g] = key
        keycol[g] = jnp.broadcast_to(key, (128, GROUP)).T
        for u in range(per_group):
            t = g * per_group + u
            if t != SELF:
                data_copy(t).wait_recv()
        for k in range(g):
            score(g, k)
            score(k, g)
        score(g, g)

    rstage[...] = jnp.zeros_like(rstage)
    rrecv[SELF] = jnp.zeros_like(rrecv[SELF])
    for g in range(groups):
        value = best[g]
        for u in range(per_group):
            t = g * per_group + u
            piece = value[:, u * slot : (u + 1) * slot]
            if t == SELF:
                rrecv[t, :, 0:slot] = piece
            else:
                rstage[t, :, 0:slot] = piece
                result_copy(t).start()

    hot_pos = jnp.where(
        lax.broadcasted_iota(jnp.int32, (128, rows), 0) == pos, 1.0, 0.0
    ).astype(jnp.bfloat16)
    hot_step = lax.broadcasted_iota(jnp.int32, (n, rows), 0) == step_row
    for t in others:
        result_copy(t).wait_recv()
    back = rrecv[:, 0, :]
    high = back.astype(jnp.bfloat16)
    rest = back - high.astype(jnp.float32)
    mid = rest.astype(jnp.bfloat16)
    low = (rest - mid.astype(jnp.float32)).astype(jnp.bfloat16)
    spread = jnp.dot(
        jnp.concatenate([high, mid, low], axis=0), hot_pos, preferred_element_type=jnp.float32
    )
    spread = (spread[0:n] + spread[n : 2 * n]) + spread[2 * n :]
    result = jnp.sum(jnp.where(hot_step, spread, 0.0), axis=0, keepdims=True)
    for k in range(chunks):
        out_ref[k : k + 1, :] = result[:, k * 128 : (k + 1) * 128]
    for t in others:
        meta_copy(t).wait_send()
        data_copy(t).wait_send()
        result_copy(t).wait_send()


def shards(embeddings, cluster_id, member_rank):
    rows, width = embeddings.shape
    n_src = lax.axis_size("src")
    n_own = lax.axis_size("own")
    n = n_src * n_own
    slot = -(-(rows // n) // 16) * 16
    groups = n * slot // GROUP
    f32, bf16 = jnp.float32, jnp.bfloat16
    out = pl.pallas_call(
        functools.partial(kernel, n_src, n_own, slot),
        out_shape=jax.ShapeDtypeStruct((rows // 128, 128), f32),
        in_specs=[
            pl.BlockSpec(memory_space=pl.ANY),
            pl.BlockSpec(memory_space=pltpu.VMEM),
            pl.BlockSpec(memory_space=pltpu.VMEM),
        ],
        out_specs=pl.BlockSpec(memory_space=pltpu.VMEM),
        scratch_shapes=[
            pltpu.VMEM((rows, width), bf16),
            pltpu.VMEM((n * slot, width), bf16),
            pltpu.VMEM((n * slot, width), bf16),
            pltpu.VMEM((n, 2, 128), f32),
            pltpu.VMEM((n, 2, 128), f32),
            pltpu.VMEM((n, 1, 128), f32),
            pltpu.VMEM((n, 1, 128), f32),
            pltpu.VMEM((groups, 1, GROUP), f32),
            pltpu.VMEM((groups, 1, GROUP), f32),
            pltpu.VMEM((groups, GROUP, 128), f32),
            pltpu.VMEM((groups, 1, GROUP), f32),
            pltpu.SemaphoreType.DMA,
        ]
        + [pltpu.SemaphoreType.DMA((n,))] * 6,
        compiler_params=pltpu.CompilerParams(
            collective_id=0, has_side_effects=True, vmem_limit_bytes=40 * 1024 * 1024
        ),
    )(embeddings, cluster_id.reshape(rows // 128, 128), member_rank.reshape(rows // 128, 128))
    return out.reshape(rows)


def solution(mesh):
    in_specs = (
        P(("groups", "src", "own"), None),
        P(("groups", "src", "own")),
        P(("groups", "src", "own")),
    )
    out_specs = P(("groups", "src", "own"))
    return jax.shard_map(shards, mesh=mesh, in_specs=in_specs, out_specs=out_specs, check_vma=False)
```

time: 105 us -> 51.3 us (0.49)
  Pallas kernels: 0 us -> 47.7 us
  waiting for transfers between devices: 29.8 us -> 0 us
  starting transfers between devices: 19.4 us -> 0 us
  local copies, waits for them, and re-layouts: 21 us -> 3.38 us
  other arithmetic: 16.8 us -> 0 us
  blocking collectives: 15.3 us -> 0 us
  matrix products: 2.31 us -> 0 us
    pallas_call x0 -> x1, Pallas kernels: none -> 47.7 us  [shards(): pl.pallas_call(functools.partial(kernel, n_src, n_own, slot), out_shape=j...]
    all_to_all x3 -> x0, waiting for transfers between devices: 29.8 us -> none  [the longest x1 29.8 us: shards(): lax.all_to_all(outgoing.reshape(owners, slot_rows, width), ('src', 'own')...]
    all_to_all x3 -> x0, starting transfers between devices: 19.4 us -> none  [the longest x1 7.36 us: shards(): lax.all_to_all(ids_out.reshape(owners, slot_rows), ('src', 'own'), split_...]
    all_to_all x1 -> x0, blocking collectives: 15.3 us -> none  [shards(): lax.all_to_all(largest.reshape(owners, slot_rows), ('src', 'own'), split_...]
    scatter x2 -> x0, local copies, waits for them, and re-layouts: 8.94 us -> none  [the longest x1 4.47 us: shards(): rank_out = jnp.full((capacity,), -1, jnp.int32).at[target].set(member_rank)]
    gather x1 -> x0, local copies, waits for them, and re-layouts: 8.83 us -> none  [shards(): return returned.reshape(capacity)[target]]
    scatter x1 -> x0, other arithmetic: 6.87 us -> none  [shards(): jnp.zeros((capacity, width), jnp.bfloat16).at[target].set(normalized)]
    another operation x3 -> x0, other arithmetic: 4.63 us -> none
  transfers between devices with their start and end apart: 3 -> 0, of which waited for: 1 -> 0; matrix products, arithmetic and copies ran while one was open for 15% -> 0% of each run, Pallas kernels for 0% -> 0%
where the time goes in v1:
time: 51.3 us; the launch traced here: 51.1 us
  Pallas kernels  47.7 us (93%)
  local copies, waits for them, and re-layouts  3.38 us (7%)
    pallas_call x1, Pallas kernels, shards(): pl.pallas_call(functools.partial(kernel, n_src, n_own, slot), out_shape=j...  47.7 us
    unnamed x7, local copies, waits for them, and re-layouts  3.38 us

profile of v1, /device:TPU:0, one launch (start us, length us, event | category | flops | bytes accessed | tf_op | source)
XLA Modules:
  0.0 51.1 jit_solution(4087862319748061772)
XLA Ops:
  0.0 0.0 copy-start
  0.0 1.4 %copy-done = bf16[1024,768]{1,0:T(8,128)(2,1)S(1)} copy-done((bf16[1024,768]{1,0:T(8,128)(2,1)S(1)}, bf16[1024,768]{1,0:T(8,128)(2,1)}, u32[]{:S(2)}) %copy-start) | copy-done | bytes 1572888
  1.4 0.0 copy-start.1
  1.4 0.7 %copy-done.1 = s32[1024]{0:T(1024)S(1)} copy-done((s32[1024]{0:T(1024)S(1)}, s32[1024]{0:T(1024)}, u32[]{:S(2)}) %copy-start.1) | copy-done | bytes 4120
  2.1 0.0 copy-start.2
  2.1 0.7 %copy-done.2 = s32[1024]{0:T(1024)S(1)} copy-done((s32[1024]{0:T(1024)S(1)}, s32[1024]{0:T(1024)}, u32[]{:S(2)}) %copy-start.2) | copy-done | bytes 4120
  2.8 47.7 %shard_map.37 = f32[8,128]{1,0:T(8,128)S(1)} custom-call(bf16[1024,768]{1,0:T(8,128)(2,1)S(1)} %copy-done, s32[8,128]{1,0:T(8,128)S(1)} %bitcast.4, s32[8,128]{1,0:T(8,128)S(1)} %bitcast.5), custom_call_target="tpu_custom_call" | custom-call | tf_op jit(solution)/shard_map/pallas_call | solution.py:215
  50.5 0.6 %copy.5 = f32[1024]{0:T(1024)} copy(f32[1024]{0:T(1024)S(1)} %bitcast.3) | data formatting | bytes 8192
Async XLA Ops:
  0.0 1.4 %copy-start = (bf16[1024,768]{1,0:T(8,128)(2,1)S(1)}, bf16[1024,768]{1,0:T(8,128)(2,1)}, u32[]{:S(2)}) copy-start(bf16[1024,768]{1,0:T(8,128)(2,1)} %emb_hbm.1) | copy-start | bytes 4718596
  1.4 0.7 %copy-start.1 = (s32[1024]{0:T(1024)S(1)}, s32[1024]{0:T(1024)}, u32[]{:S(2)}) copy-start(s32[1024]{0:T(1024)} %param.4) | copy-start | bytes 12292
  2.1 0.7 %copy-start.2 = (s32[1024]{0:T(1024)S(1)}, s32[1024]{0:T(1024)}, u32[]{:S(2)}) copy-start(s32[1024]{0:T(1024)} %param.5) | copy-start | bytes 12292

commit v2 on v1

--- a/solution.py
+++ b/solution.py
@@ -11,7 +11,10 @@
 MESH = pl.DeviceIdType.MESH
 GROUP = 256
 GAP = 4096.0
-SELF = 1
+
+
+def plan(h, n_own):
+    return [(near, j, c) for j in range(h) for c in range(n_own) for near in (0, 1)]
 
 
 def log2(n):
@@ -20,9 +23,9 @@
 
 
 def kernel(
-    n_src, n_own, slot, emb_hbm, cid_ref, rank_ref, out_ref,
-    emb, stage, recv, mstage, mrecv, rstage, rrecv, keyrow, baserow, keycol, best,
-    in_sem, d_send, d_recv, m_send, m_recv, r_send, r_recv,
+    n_src, n_own, slot, emb_hbm, cid_hbm, rank_hbm, out_ref,
+    emb, cid_ref, rank_ref, stage, recv, mstage, mrecv, rstage, rrecv, keyrow, baserow, keycol, best,
+    in_sems, d_send, d_recv, m_send, m_recv, r_send, r_recv,
 ):
     n = n_src * n_own
     h = n_src // 2
@@ -35,26 +38,36 @@
     half, off = s // h, s % h
 
     def place(t, sign):
-        near, q = t % 2, t // 2
-        j, cc = q // n_own, q % n_own
+        near, j, cc = order[t]
         side = half if near else 1 - half
         return {
             "src": side * h + (off + h + sign * j) % h,
             "own": (c + n_own + sign * cc) % n_own,
         }
 
+    order = plan(h, n_own)
+    SELF = order.index((1, 0, 0))
     others = [t for t in range(n) if t != SELF]
-    load = pltpu.make_async_copy(emb_hbm, emb, in_sem)
-    load.start()
+    loads = [
+        pltpu.make_async_copy(src, dst, in_sems.at[i])
+        for i, (src, dst) in enumerate([(cid_hbm, cid_ref), (rank_hbm, rank_ref), (emb_hbm, emb)])
+    ]
+    for load in loads:
+        load.start()
     barrier = pltpu.get_barrier_semaphore()
     for t in others:
         pl.semaphore_signal(barrier, inc=1, device_id=place(t, 1), device_id_type=MESH)
 
+    loads[0].wait()
+    loads[1].wait()
     cid = cid_ref[...]
     owner = cid & (n - 1)
     ds, dc = owner >> log2(n_own), owner & (n_own - 1)
     near = jnp.where((ds >> log2(h)) == half, 1, 0)
-    step = 2 * ((((ds & (h - 1)) - off) & (h - 1)) * n_own + ((dc - c) & (n_own - 1))) + near
+    code = (near * h + ((ds - off) & (h - 1))) * n_own + ((dc - c) & (n_own - 1))
+    step = jnp.zeros_like(code)
+    for t, (near, j, cc) in enumerate(order):
+        step = jnp.where(code == (near * h + j) * n_own + cc, t, step)
     upper = jnp.where(
         lax.broadcasted_iota(jnp.int32, (128, 128), 0) < lax.broadcasted_iota(jnp.int32, (128, 128), 1),
         1.0, 0.0,
@@ -103,7 +116,7 @@
             device_id=place(t, -1), device_id_type=MESH,
         )
 
-    load.wait()
+    loads[2].wait()
     for g in range(groups):
         slots = lax.broadcasted_iota(jnp.int32, (GROUP, rows), 0) + g * GROUP
         pick = jnp.where(slots == target, 1.0, 0.0).astype(jnp.bfloat16)
@@ -216,13 +229,15 @@
         functools.partial(kernel, n_src, n_own, slot),
         out_shape=jax.ShapeDtypeStruct((rows // 128, 128), f32),
         in_specs=[
-            pl.BlockSpec(memory_space=pl.ANY),
-            pl.BlockSpec(memory_space=pltpu.VMEM),
-            pl.BlockSpec(memory_space=pltpu.VMEM),
+            pl.BlockSpec(memory_space=pltpu.HBM),
+            pl.BlockSpec(memory_space=pltpu.HBM),
+            pl.BlockSpec(memory_space=pltpu.HBM),
         ],
         out_specs=pl.BlockSpec(memory_space=pltpu.VMEM),
         scratch_shapes=[
             pltpu.VMEM((rows, width), bf16),
+            pltpu.VMEM((rows // 128, 128), jnp.int32),
+            pltpu.VMEM((rows // 128, 128), jnp.int32),
             pltpu.VMEM((n * slot, width), bf16),
             pltpu.VMEM((n * slot, width), bf16),
             pltpu.VMEM((n, 2, 128), f32),
@@ -233,11 +248,11 @@
             pltpu.VMEM((groups, 1, GROUP), f32),
             pltpu.VMEM((groups, GROUP, 128), f32),
             pltpu.VMEM((groups, 1, GROUP), f32),
-            pltpu.SemaphoreType.DMA,
+            pltpu.SemaphoreType.DMA((3,)),
         ]
         + [pltpu.SemaphoreType.DMA((n,))] * 6,
         compiler_params=pltpu.CompilerParams(
-            collective_id=0, has_side_effects=True, vmem_limit_bytes=40 * 1024 * 1024
+            collective_id=0, has_side_effects=True, vmem_limit_bytes=60 * 1024 * 1024
         ),
     )(embeddings, cluster_id.reshape(rows // 128, 128), member_rank.reshape(rows // 128, 128))
     return out.reshape(rows)

time: 51.3 us -> 49.7 us (0.969)
  local copies, waits for them, and re-layouts: 3.38 us -> 1.28 us
    unnamed x7 -> x1, local copies, waits for them, and re-layouts: 3.38 us -> 1.28 us
where the time goes in v2:
time: 49.7 us; the launch traced here: 49.5 us
  Pallas kernels  48.2 us (97%)
  local copies, waits for them, and re-layouts  1.28 us (3%)
    pallas_call x1, Pallas kernels, shards(): pl.pallas_call(functools.partial(kernel, n_src, n_own, slot), out_shape=j...  48.2 us
    unnamed x1, local copies, waits for them, and re-layouts  1.28 us

profile of v2, /device:TPU:0, one launch (start us, length us, event | category | flops | bytes accessed | tf_op | source)
XLA Modules:
  0.0 49.5 jit_solution(2561571911571018088)
XLA Ops:
  0.0 48.2 %shard_map.37 = f32[8,128]{1,0:T(8,128)} custom-call(bf16[1024,768]{1,0:T(8,128)(2,1)} %emb_hbm.1, s32[8,128]{1,0:T(8,128)} %bitcast.4, s32[8,128]{1,0:T(8,128)} %bitcast.5), custom_call_target="tpu_custom_call" | custom-call | tf_op jit(solution)/shard_map/pallas_call | solution.py:228
  48.2 1.3 %copy.5 = f32[1024]{0:T(1024)} copy(f32[1024]{0:T(1024)} %bitcast.3) | data formatting | bytes 8192

commit v3 on v2

--- a/solution.py
+++ b/solution.py
@@ -227,7 +227,7 @@
     f32, bf16 = jnp.float32, jnp.bfloat16
     out = pl.pallas_call(
         functools.partial(kernel, n_src, n_own, slot),
-        out_shape=jax.ShapeDtypeStruct((rows // 128, 128), f32),
+        out_shape=pltpu.VMEM((rows // 128, 128), f32),
         in_specs=[
             pl.BlockSpec(memory_space=pltpu.HBM),
             pl.BlockSpec(memory_space=pltpu.HBM),

time: 49.7 us -> 48.4 us (0.974)
  local copies, waits for them, and re-layouts: 1.28 us -> 0.6 us
  Pallas kernels: 48.2 us -> 47.6 us
    unnamed x1, local copies, waits for them, and re-layouts: 1.28 us -> 0.6 us
    pallas_call x1, Pallas kernels: 48.2 us -> 47.6 us  [shards(): pl.pallas_call(functools.partial(kernel, n_src, n_own, slot), out_shape=p...]
where the time goes in v3:
time: 48.4 us; the launch traced here: 48.2 us
  Pallas kernels  47.6 us (98%)
  local copies, waits for them, and re-layouts  0.6 us (1%)
    pallas_call x1, Pallas kernels, shards(): pl.pallas_call(functools.partial(kernel, n_src, n_own, slot), out_shape=p...  47.6 us

profile of v3, /device:TPU:0, one launch (start us, length us, event | category | flops | bytes accessed | tf_op | source)
XLA Modules:
  0.0 48.2 jit_solution(9392769209745384382)
XLA Ops:
  0.0 47.6 %shard_map.37 = f32[8,128]{1,0:T(8,128)S(1)} custom-call(bf16[1024,768]{1,0:T(8,128)(2,1)} %emb_hbm.1, s32[8,128]{1,0:T(8,128)} %bitcast.4, s32[8,128]{1,0:T(8,128)} %bitcast.5), custom_call_target="tpu_custom_call" | custom-call | tf_op jit(solution)/shard_map/pallas_call | solution.py:228
  47.6 0.6 %copy.5 = f32[1024]{0:T(1024)} copy(f32[1024]{0:T(1024)S(1)} %bitcast.3) | data formatting | bytes 8192

commit v4 on v3

--- a/solution.py
+++ b/solution.py
@@ -14,7 +14,7 @@
 
 
 def plan(h, n_own):
-    return [(near, j, c) for j in range(h) for c in range(n_own) for near in (0, 1)]
+    return [(near, j, c) for j in range(h) for c in range(n_own) for near in (1, 0)]
 
 
 def log2(n):
@@ -24,7 +24,7 @@
 
 def kernel(
     n_src, n_own, slot, emb_hbm, cid_hbm, rank_hbm, out_ref,
-    emb, cid_ref, rank_ref, stage, recv, mstage, mrecv, rstage, rrecv, keyrow, baserow, keycol, best,
+    emb, cid_ref, rank_ref, stage, recv, mstage, mrecv, rstage, rrecv, keyrow, baserow, keycol, best, hot_pos, hot_step,
     in_sems, d_send, d_recv, m_send, m_recv, r_send, r_recv,
 ):
     n = n_src * n_own
@@ -46,8 +46,10 @@
         }
 
     order = plan(h, n_own)
-    SELF = order.index((1, 0, 0))
-    others = [t for t in range(n) if t != SELF]
+    SELF = 0
+    others = range(1, n)
+    to = [place(t, 1) for t in range(n)]
+    back_to = [place(t, -1) for t in range(n)]
     loads = [
         pltpu.make_async_copy(src, dst, in_sems.at[i])
         for i, (src, dst) in enumerate([(cid_hbm, cid_ref), (rank_hbm, rank_ref), (emb_hbm, emb)])
@@ -56,7 +58,7 @@
         load.start()
     barrier = pltpu.get_barrier_semaphore()
     for t in others:
-        pl.semaphore_signal(barrier, inc=1, device_id=place(t, 1), device_id_type=MESH)
+        pl.semaphore_signal(barrier, inc=1, device_id=to[t], device_id_type=MESH)
 
     loads[0].wait()
     loads[1].wait()
@@ -100,21 +102,29 @@
     def data_copy(t):
         part = pl.ds(t * slot, slot)
         return pltpu.make_async_remote_copy(
-            src_ref=stage.at[part], dst_ref=recv.at[part], send_sem=d_send.at[t], recv_sem=d_recv.at[t],
-            device_id=place(t, 1), device_id_type=MESH,
+            src_ref=stage.at[part], dst_ref=recv.at[part], send_sem=d_send.at[t // per_group], recv_sem=d_recv.at[t // per_group],
+            device_id=to[t], device_id_type=MESH,
         )
 
     def meta_copy(t):
         return pltpu.make_async_remote_copy(
-            src_ref=mstage.at[t], dst_ref=mrecv.at[t], send_sem=m_send.at[t], recv_sem=m_recv.at[t],
-            device_id=place(t, 1), device_id_type=MESH,
+            src_ref=mstage.at[t], dst_ref=mrecv.at[t], send_sem=m_send, recv_sem=m_recv.at[t // per_group],
+            device_id=to[t], device_id_type=MESH,
         )
 
     def result_copy(t):
         return pltpu.make_async_remote_copy(
-            src_ref=rstage.at[t], dst_ref=rrecv.at[t], send_sem=r_send.at[t], recv_sem=r_recv.at[t],
-            device_id=place(t, -1), device_id_type=MESH,
-        )
+            src_ref=rstage.at[t], dst_ref=rrecv.at[t], send_sem=r_send, recv_sem=r_recv,
+            device_id=back_to[t], device_id_type=MESH,
+        )
+
+    def settle(ref, first, count, sem):
+        part = ref.at[pl.ds(first, count)]
+        pltpu.make_async_copy(part, part, sem).wait()
+
+    def span(g):
+        first = max(g * per_group, 1)
+        return first, (g + 1) * per_group - first
 
     loads[2].wait()
     for g in range(groups):
@@ -144,6 +154,14 @@
                 meta_copy(t).start()
                 data_copy(t).start()
 
+    hot_pos[...] = jnp.where(
+        lax.broadcasted_iota(jnp.int32, (128, rows), 0) == pos, 1.0, 0.0
+    ).astype(jnp.bfloat16)
+    hot_step[...] = jnp.where(
+        lax.broadcasted_iota(jnp.int32, (n, rows), 0) == step_row, 1.0, 0.0
+    )
+    rstage[...] = jnp.zeros_like(rstage)
+    rrecv[SELF] = jnp.zeros_like(rrecv[SELF])
     best[...] = jnp.full_like(best, -1.0)
 
     def score(k, q):
@@ -159,11 +177,11 @@
         )
 
     for g in range(groups):
+        first, count = span(g)
+        settle(mrecv, first, count, m_recv.at[g])
         pieces = []
         for u in range(per_group):
             t = g * per_group + u
-            if t != SELF:
-                meta_copy(t).wait_recv()
             pieces.append(mrecv[t, :, 0:slot])
         pieces = jnp.concatenate(pieces, axis=1)
         base = pieces[0:1] * GAP
@@ -171,17 +189,16 @@
         baserow[g] = base
         keyrow[g] = key
         keycol[g] = jnp.broadcast_to(key, (128, GROUP)).T
-        for u in range(per_group):
-            t = g * per_group + u
-            if t != SELF:
-                data_copy(t).wait_recv()
+        if g == groups - 1:
+            settle(mstage, 1, n - 1, m_send)
+            for k in range(g):
+                settle(stage, span(k)[0] * slot, span(k)[1] * slot, d_send.at[k])
+        settle(recv, first * slot, count * slot, d_recv.at[g])
         for k in range(g):
             score(g, k)
             score(k, g)
         score(g, g)
 
-    rstage[...] = jnp.zeros_like(rstage)
-    rrecv[SELF] = jnp.zeros_like(rrecv[SELF])
     for g in range(groups):
         value = best[g]
         for u in range(per_group):
@@ -191,30 +208,23 @@
                 rrecv[t, :, 0:slot] = piece
             else:
                 rstage[t, :, 0:slot] = piece
-                result_copy(t).start()
-
-    hot_pos = jnp.where(
-        lax.broadcasted_iota(jnp.int32, (128, rows), 0) == pos, 1.0, 0.0
-    ).astype(jnp.bfloat16)
-    hot_step = lax.broadcasted_iota(jnp.int32, (n, rows), 0) == step_row
     for t in others:
-        result_copy(t).wait_recv()
+        result_copy(t).start()
+    settle(stage, span(groups - 1)[0] * slot, span(groups - 1)[1] * slot, d_send.at[groups - 1])
+    settle(rstage, 1, n - 1, r_send)
+    settle(rrecv, 1, n - 1, r_recv)
     back = rrecv[:, 0, :]
     high = back.astype(jnp.bfloat16)
     rest = back - high.astype(jnp.float32)
     mid = rest.astype(jnp.bfloat16)
     low = (rest - mid.astype(jnp.float32)).astype(jnp.bfloat16)
     spread = jnp.dot(
-        jnp.concatenate([high, mid, low], axis=0), hot_pos, preferred_element_type=jnp.float32
+        jnp.concatenate([high, mid, low], axis=0), hot_pos[...], preferred_element_type=jnp.float32
     )
     spread = (spread[0:n] + spread[n : 2 * n]) + spread[2 * n :]
-    result = jnp.sum(jnp.where(hot_step, spread, 0.0), axis=0, keepdims=True)
+    result = jnp.sum(hot_step[...] * spread, axis=0, keepdims=True)
     for k in range(chunks):
         out_ref[k : k + 1, :] = result[:, k * 128 : (k + 1) * 128]
-    for t in others:
-        meta_copy(t).wait_send()
-        data_copy(t).wait_send()
-        result_copy(t).wait_send()
 
 
 def shards(embeddings, cluster_id, member_rank):
@@ -248,9 +258,16 @@
             pltpu.VMEM((groups, 1, GROUP), f32),
             pltpu.VMEM((groups, GROUP, 128), f32),
             pltpu.VMEM((groups, 1, GROUP), f32),
+            pltpu.VMEM((128, rows), bf16),
+            pltpu.VMEM((n, rows), f32),
             pltpu.SemaphoreType.DMA((3,)),
-        ]
-        + [pltpu.SemaphoreType.DMA((n,))] * 6,
+            pltpu.SemaphoreType.DMA((groups,)),
+            pltpu.SemaphoreType.DMA((groups,)),
+            pltpu.SemaphoreType.DMA,
+            pltpu.SemaphoreType.DMA((groups,)),
+            pltpu.SemaphoreType.DMA,
+            pltpu.SemaphoreType.DMA,
+        ],
         compiler_params=pltpu.CompilerParams(
             collective_id=0, has_side_effects=True, vmem_limit_bytes=60 * 1024 * 1024
         ),

time: 48.4 us -> 47.6 us (0.983)
  Pallas kernels: 47.6 us -> 46.8 us
    pallas_call x1, Pallas kernels: 47.6 us -> 46.8 us  [shards(): pl.pallas_call(functools.partial(kernel, n_src, n_own, slot), out_shape=p...]
where the time goes in v4:
time: 47.6 us; the launch traced here: 47.4 us
  Pallas kernels  46.8 us (98%)
  local copies, waits for them, and re-layouts  0.6 us (1%)
    pallas_call x1, Pallas kernels, shards(): pl.pallas_call(functools.partial(kernel, n_src, n_own, slot), out_shape=p...  46.8 us

profile of v4, /device:TPU:0, one launch (start us, length us, event | category | flops | bytes accessed | tf_op | source)
XLA Modules:
  0.0 47.4 jit_solution(1382509645559729383)
XLA Ops:
  0.0 46.8 %shard_map.37 = f32[8,128]{1,0:T(8,128)S(1)} custom-call(bf16[1024,768]{1,0:T(8,128)(2,1)} %emb_hbm.1, s32[8,128]{1,0:T(8,128)} %bitcast.4, s32[8,128]{1,0:T(8,128)} %bitcast.5), custom_call_target="tpu_custom_call" | custom-call | tf_op jit(solution)/shard_map/pallas_call | solution.py:238
  46.8 0.6 %copy.5 = f32[1024]{0:T(1024)} copy(f32[1024]{0:T(1024)S(1)} %bitcast.3) | data formatting | bytes 8192
